TPU v7x, 512 devices: a whole 4x8x8 slice. The times are simulated.
512 devices in a mesh: dp: 32 (over z, y_hi), tensor: 16 (over x, y_lo, core).
Axes of the slice: x: 4, y: 8 (y_hi: 4, y_lo: 2; y = y_hi * 2 + y_lo), z: 8, core: 2. Of those that a mesh axis runs over, the one named last changes fastest.
Arguments:
- tokens: bfloat16 [512, 8192], P('dp', 'tensor'), may hold values from -6 to 6
- out_grad: bfloat16 [512, 8192], P('dp', 'tensor'), may hold values from -6 to 6
- gate_weight: bfloat16 [8192, 14336], P('tensor', 'dp'), may hold values from -0.0625 to 0.0625
- up_weight: bfloat16 [8192, 14336], P('tensor', 'dp'), may hold values from -0.0625 to 0.0625
- down_weight: bfloat16 [14336, 8192], P('dp', 'tensor'), may hold values from -0.0625 to 0.0625
- pair_list: int32 [512, 2], P(('dp', 'tensor')), may hold values from 0 to 31, as said below
Outputs:
- act_cov: float32 [512, 448, 448], P(('dp', 'tensor'))
- grad_cov: float32 [512, 448, 448], P(('dp', 'tensor'))
Inputs may be any that keep to these rules, and one draw needn't show every extreme that they name: `pair_list`: row 16 * i + j is (i, (i + e_j) mod 32), where e is one permutation of 1 to 16 shared by every i.
All inputs are finite; a program needn't handle non-finite values.
Results may differ from a plain program's by a relative error of at most 0.004.
Values may be sent and summed in bfloat16 or wider, within the bound.
A program may use at most 64 MiB of HBM per device.

v0:
```python
import jax
import jax.numpy as jnp
from jax import lax
from jax.sharding import PartitionSpec as P


def passed_along(value, axis, steps):
    count = lax.axis_size(axis)
    pairs = [(source, (source + steps) % count) for source in range(count)]
    return lax.ppermute(value, axis, pairs)


def gram_of(left_block, right_block):
    return lax.dot_general(
        left_block, right_block, (((0,), (0,)), ((), ())), preferred_element_type=jnp.float32
    )


def activate(summed, block_width):
    gate_sum = summed[:, :block_width]
    up_sum = summed[:, block_width : 2 * block_width]
    grad_sum = summed[:, 2 * block_width :]
    return ((jax.nn.silu(gate_sum) * up_sum).astype(jnp.bfloat16), grad_sum.astype(jnp.bfloat16))


def diagonal_tile(own_block, far_block, upper_mask):
    return jnp.where(upper_mask, gram_of(own_block, own_block), gram_of(far_block, far_block))


def local(tokens, out_grad, gate_weight, up_weight, down_weight, pair_list):
    block_width = gate_weight.shape[1]
    token_rows, grad_rows = (
        lax.all_gather(tokens, "dp", axis=0, tiled=True),
        lax.all_gather(out_grad, "dp", axis=0, tiled=True),
    )
    token_count = token_rows.shape[0]
    gate_term = jnp.dot(token_rows, gate_weight, preferred_element_type=jnp.float32)
    up_term = jnp.dot(token_rows, up_weight, preferred_element_type=jnp.float32)
    grad_term = lax.dot_general(
        grad_rows, down_weight, (((1,), (1,)), ((), ())), preferred_element_type=jnp.float32
    )
    summed = lax.psum_scatter(
        jnp.concatenate([gate_term, up_term, grad_term], axis=1),
        "tensor",
        scatter_dimension=0,
        tiled=True,
    )
    act_share, grad_share = activate(summed, block_width)
    own_act, own_grad = (
        lax.all_gather(act_share, "tensor", axis=0, tiled=True),
        lax.all_gather(grad_share, "tensor", axis=0, tiled=True),
    )
    cycle_size = lax.axis_size("dp")
    dp_index = lax.axis_index("dp")
    distance = (pair_list[0, 1] - dp_index) % cycle_size
    far_act, far_grad = (own_act, own_grad)
    for bit_index in range(lax.axis_size("tensor").bit_length()):
        shifted_act, shifted_grad = passed_along((far_act, far_grad), "dp", -(1 << bit_index))
        chosen = distance >> bit_index & 1 == 1
        far_act = jnp.where(chosen, shifted_act, far_act)
        far_grad = jnp.where(chosen, shifted_grad, far_grad)
    diagonal = (distance == cycle_size // 2) & (dp_index >= cycle_size // 2)
    inverse = 1.0 / token_count
    row_ids = lax.broadcasted_iota(jnp.int32, (block_width, block_width), 0)
    col_ids = lax.broadcasted_iota(jnp.int32, (block_width, block_width), 1)
    upper_mask = row_ids <= col_ids

    def cross_tiles(own_act, far_act, own_grad, far_grad):
        return (gram_of(own_act, far_act) * inverse, gram_of(own_grad, far_grad) * inverse)

    def diagonal_tiles(own_act, far_act, own_grad, far_grad):
        return (
            diagonal_tile(own_act, far_act, upper_mask) * inverse,
            diagonal_tile(own_grad, far_grad, upper_mask) * inverse,
        )

    act_tile, grad_tile = lax.cond(
        diagonal, diagonal_tiles, cross_tiles, own_act, far_act, own_grad, far_grad
    )
    return (act_tile[None], grad_tile[None])


def solution(mesh):
    in_specs = (
        P("dp", "tensor"),
        P("dp", "tensor"),
        P("tensor", "dp"),
        P("tensor", "dp"),
        P("dp", "tensor"),
        P(("dp", "tensor"), None),
    )
    out_specs = (P(("dp", "tensor"), None, None), P(("dp", "tensor"), None, None))
    return jax.shard_map(local, mesh=mesh, in_specs=in_specs, out_specs=out_specs, check_vma=False)
```

profile of v0, /device:TPU:177, one launch (start us, length us, event | category | flops | bytes accessed | tf_op | source)
XLA Modules:
  0.0 547.9 jit_solution(13699379931927881690)
XLA Ops:
  7.2 61.8 %all_gather.12 = bf16[512,512]{1,0:T(8,128)(2,1)S(1)} all-gather(bf16[16,512]{1,0:T(8,128)(2,1)} %param.8), channel_id=1, replica_groups=mesh['dp'=32,'tensor'=16] {'dp'}, dimensions={0}, use_global_device_ids=true | all-gather | bytes 540672 | tf_op jit(solution)/shard_map/all_gather | solution.py:33
  69.0 67.7 %all_gather.13 = bf16[512,512]{1,0:T(8,128)(2,1)S(1)} all-gather(bf16[16,512]{1,0:T(8,128)(2,1)} %param.9), channel_id=1, replica_groups=mesh['dp'=32,'tensor'=16] {'dp'}, dimensions={0}, use_global_device_ids=true | all-gather | bytes 540672 | tf_op jit(solution)/shard_map/all_gather | solution.py:34
  136.7 0.4 fusion.10
  137.1 0.4 fusion.9
  138.3 2.2 copy.25
  140.5 100.6 %reduce-scatter.4.cloned.1.call-done = f32[32,1344]{1,0:T(8,128)} async-done(((f32[512,1344]{1,0:T(8,128)}), f32[32,1344]{1,0:T(8,128)}) %reduce-scatter.4.cloned.1.call-update) | async-done | bytes 172048 | tf_op jit(solution)/shard_map/reduce_scatter | solution.py:42
  241.1 1.1 fusion.6
  242.2 21.8 %all_gather.14 = bf16[512,448]{1,0:T(8,128)(2,1)S(1)} all-gather(bf16[32,448]{1,0:T(8,128)(2,1)S(1)} %fusion.6), channel_id=1, replica_groups=mesh['dp'=32,'tensor'=16] {'tensor'}, dimensions={0}, use_global_device_ids=true | all-gather | bytes 487424 | tf_op jit(solution)/shard_map/all_gather | solution.py:50
  264.0 4.0 collective-permute-start
  268.0 0.8 slice.19
  269.1 36.1 %all_gather.15 = bf16[512,448]{1,0:T(8,128)(2,1)S(1)} all-gather(bf16[32,448]{1,0:T(8,128)(2,1)S(1)} %copy.24), channel_id=1, replica_groups=mesh['dp'=32,'tensor'=16] {'tensor'}, dimensions={0}, use_global_device_ids=true | all-gather | bytes 487424 | tf_op jit(solution)/shard_map/all_gather | solution.py:51
  305.2 2.6 collective-permute-start.5
  307.7 0.6 slice.13
  309.1 4.2 collective-permute-start.1
  313.3 13.8 %collective-permute-done.5 = bf16[512,448]{1,0:T(8,128)(2,1)} collective-permute-done((bf16[512,448]{1,0:T(8,128)(2,1)S(1)}, bf16[512,448]{1,0:T(8,128)(2,1)}, u32[]{:S(2)}, u32[]{:S(2)}) %collective-permute-start.5) | collective-permute-done | bytes 458784 | tf_op jit(solution)/shard_map/ppermute | solution.py:10
  327.2 1.9 collective-permute-start.6
  329.1 10.2 %collective-permute-done.1 = bf16[512,448]{1,0:T(8,128)(2,1)} collective-permute-done((bf16[512,448]{1,0:T(8,128)(2,1)S(1)}, bf16[512,448]{1,0:T(8,128)(2,1)}, u32[]{:S(2)}, u32[]{:S(2)}) %collective-permute-start.1) | collective-permute-done | bytes 458784 | tf_op jit(solution)/shard_map/ppermute | solution.py:10
  339.4 5.7 %collective-permute-start.2 = (bf16[512,448]{1,0:T(8,128)(2,1)S(1)}, bf16[512,448]{1,0:T(8,128)(2,1)}, u32[]{:S(2)}, u32[]{:S(2)}) collective-permute-start(bf16[512,448]{1,0:T(8,128)(2,1)S(1)} %broadcast_select_fusion.3), channel_id=1, source_target_pairs={{0,448},{16,464},{32,480},{48,496},{64,0},{80,16},{96,32},{112,48}... | collective-permute-start | bytes 1376264 | tf_op jit(solution)/shard_map/ppermute | solution.py:10
  345.1 4.3 collective-permute-done.6
  349.4 31.8 %collective-permute-start.7 = (bf16[512,448]{1,0:T(8,128)(2,1)S(1)}, bf16[512,448]{1,0:T(8,128)(2,1)}, u32[]{:S(2)}, u32[]{:S(2)}) collective-permute-start(bf16[512,448]{1,0:T(8,128)(2,1)S(1)} %broadcast_select_fusion.2), channel_id=1, source_target_pairs={{0,448},{16,464},{32,480},{48,496},{64,0},{80,16},{96,32},{112,48}... | collective-permute-start | bytes 1376264 | tf_op jit(solution)/shard_map/ppermute | solution.py:10
  381.2 23.3 %collective-permute-start.3 = (bf16[512,448]{1,0:T(8,128)(2,1)S(1)}, bf16[512,448]{1,0:T(8,128)(2,1)}, u32[]{:S(2)}, u32[]{:S(2)}) collective-permute-start(bf16[512,448]{1,0:T(8,128)(2,1)S(1)} %broadcast_select_fusion.5), channel_id=1, source_target_pairs={{0,384},{16,400},{32,416},{48,432},{64,448},{80,464},{96,480},{112... | collective-permute-start | bytes 1376264 | tf_op jit(solution)/shard_map/ppermute | solution.py:10
  404.6 12.5 %collective-permute-start.8 = (bf16[512,448]{1,0:T(8,128)(2,1)S(1)}, bf16[512,448]{1,0:T(8,128)(2,1)}, u32[]{:S(2)}, u32[]{:S(2)}) collective-permute-start(bf16[512,448]{1,0:T(8,128)(2,1)S(1)} %broadcast_select_fusion.4), channel_id=1, source_target_pairs={{0,384},{16,400},{32,416},{48,432},{64,448},{80,464},{96,480},{112... | collective-permute-start | bytes 1376264 | tf_op jit(solution)/shard_map/ppermute | solution.py:10
  417.1 11.6 %collective-permute-done.3 = bf16[512,448]{1,0:T(8,128)(2,1)} collective-permute-done((bf16[512,448]{1,0:T(8,128)(2,1)S(1)}, bf16[512,448]{1,0:T(8,128)(2,1)}, u32[]{:S(2)}, u32[]{:S(2)}) %collective-permute-start.3) | collective-permute-done | bytes 458784 | tf_op jit(solution)/shard_map/ppermute | solution.py:10
  428.9 11.1 %collective-permute-start.4 = (bf16[512,448]{1,0:T(8,128)(2,1)S(1)}, bf16[512,448]{1,0:T(8,128)(2,1)}, u32[]{:S(2)}, u32[]{:S(2)}) collective-permute-start(bf16[512,448]{1,0:T(8,128)(2,1)S(1)} %broadcast_select_fusion.7), channel_id=1, source_target_pairs={{0,256},{16,272},{32,288},{48,304},{64,320},{80,336},{96,352},{112... | collective-permute-start | bytes 1376264 | tf_op jit(solution)/shard_map/ppermute | solution.py:10
  439.9 70.0 %collective-permute-done.8 = bf16[512,448]{1,0:T(8,128)(2,1)} collective-permute-done((bf16[512,448]{1,0:T(8,128)(2,1)S(1)}, bf16[512,448]{1,0:T(8,128)(2,1)}, u32[]{:S(2)}, u32[]{:S(2)}) %collective-permute-start.8) | collective-permute-done | bytes 458784 | tf_op jit(solution)/shard_map/ppermute | solution.py:10
  510.0 1.9 collective-permute-start.9
  511.9 1.1 broadcast_select_fusion.9
  513.0 24.0 %collective-permute-done.9 = bf16[512,448]{1,0:T(8,128)(2,1)} collective-permute-done((bf16[512,448]{1,0:T(8,128)(2,1)S(1)}, bf16[512,448]{1,0:T(8,128)(2,1)}, u32[]{:S(2)}, u32[]{:S(2)}) %collective-permute-start.9) | collective-permute-done | bytes 458784 | tf_op jit(solution)/shard_map/ppermute | solution.py:10
  537.0 1.1 broadcast_select_fusion.8
  538.3 2.7 conditional.1
  538.3 1.4 fusion.1
  539.7 1.4 fusion
  (28 shorter events, 1.6 us)
Async XLA Ops:
  7.2 129.5 %copy-start = (bf16[512,448]{0,1:T(8,128)(2,1)S(1)}, bf16[512,448]{0,1:T(8,128)(2,1)}, u32[]{:S(2)}) copy-start(bf16[512,448]{0,1:T(8,128)(2,1)} %param.11) | copy-start | bytes 1376260
  7.2 129.9 %copy-start.1 = (bf16[512,448]{0,1:T(8,128)(2,1)S(1)}, bf16[512,448]{0,1:T(8,128)(2,1)}, u32[]{:S(2)}) copy-start(bf16[512,448]{0,1:T(8,128)(2,1)} %param.10) | copy-start | bytes 1376260
  7.2 130.4 %copy-start.2 = (bf16[448,512]{1,0:T(8,128)(2,1)S(1)}, bf16[448,512]{1,0:T(8,128)(2,1)}, u32[]{:S(2)}) copy-start(bf16[448,512]{1,0:T(8,128)(2,1)} %param.12) | copy-start | bytes 1376260
  7.2 233.9 %reduce-scatter.4.cloned.1.call-start = ((), (), s32[]{:S(2)}) async-start(), calls=%async_computation.1 | async-start | bytes 3063808 | tf_op jit(solution)/shard_map/reduce_scatter | solution.py:42
  140.5 167.2 %copy-start.3 = (s32[1,2]{1,0:T(1,128)S(1)}, s32[1,2]{1,0:T(1,128)}, u32[]{:S(2)}) copy-start(s32[1,2]{1,0:T(1,128)} %param.13) | copy-start | bytes 28
  264.0 45.0 %collective-permute-start = (bf16[512,448]{1,0:T(8,128)(2,1)S(1)}, bf16[512,448]{1,0:T(8,128)(2,1)S(1)}, u32[]{:S(2)}, u32[]{:S(2)}) collective-permute-start(bf16[512,448]{1,0:T(8,128)(2,1)S(1)} %all_gather.14), channel_id=1, source_target_pairs={{0,496},{16,0},{32,16},{48,32},{64,48},{80,64},{96,80},{112,96},{1... | collective-permute-start | bytes 1376264 | tf_op jit(solution)/shard_map/ppermute | solution.py:10
  305.2 22.0 %collective-permute-start.5 = (bf16[512,448]{1,0:T(8,128)(2,1)S(1)}, bf16[512,448]{1,0:T(8,128)(2,1)}, u32[]{:S(2)}, u32[]{:S(2)}) collective-permute-start(bf16[512,448]{1,0:T(8,128)(2,1)S(1)} %all_gather.15), channel_id=1, source_target_pairs={{0,496},{16,0},{32,16},{48,32},{64,48},{80,64},{96,80},{112,96},{1... | collective-permute-start | bytes 1376264 | tf_op jit(solution)/shard_map/ppermute | solution.py:10
  309.1 30.3 %collective-permute-start.1 = (bf16[512,448]{1,0:T(8,128)(2,1)S(1)}, bf16[512,448]{1,0:T(8,128)(2,1)}, u32[]{:S(2)}, u32[]{:S(2)}) collective-permute-start(bf16[512,448]{1,0:T(8,128)(2,1)S(1)} %broadcast_select_fusion.1), channel_id=1, source_target_pairs={{0,480},{16,496},{32,0},{48,16},{64,32},{80,48},{96,64},{112,80},{... | collective-permute-start | bytes 1376264 | tf_op jit(solution)/shard_map/ppermute | solution.py:10
  327.2 22.1 %collective-permute-start.6 = (bf16[512,448]{1,0:T(8,128)(2,1)S(1)}, bf16[512,448]{1,0:T(8,128)(2,1)}, u32[]{:S(2)}, u32[]{:S(2)}) collective-permute-start(bf16[512,448]{1,0:T(8,128)(2,1)S(1)} %broadcast_select_fusion), channel_id=1, source_target_pairs={{0,480},{16,496},{32,0},{48,16},{64,32},{80,48},{96,64},{112,80},{... | collective-permute-start | bytes 1376264 | tf_op jit(solution)/shard_map/ppermute | solution.py:10
  339.4 41.8 %collective-permute-start.2 = (bf16[512,448]{1,0:T(8,128)(2,1)S(1)}, bf16[512,448]{1,0:T(8,128)(2,1)}, u32[]{:S(2)}, u32[]{:S(2)}) collective-permute-start(bf16[512,448]{1,0:T(8,128)(2,1)S(1)} %broadcast_select_fusion.3), channel_id=1, source_target_pairs={{0,448},{16,464},{32,480},{48,496},{64,0},{80,16},{96,32},{112,48}... | collective-permute-start | bytes 1376264 | tf_op jit(solution)/shard_map/ppermute | solution.py:10
  349.4 55.1 %collective-permute-start.7 = (bf16[512,448]{1,0:T(8,128)(2,1)S(1)}, bf16[512,448]{1,0:T(8,128)(2,1)}, u32[]{:S(2)}, u32[]{:S(2)}) collective-permute-start(bf16[512,448]{1,0:T(8,128)(2,1)S(1)} %broadcast_select_fusion.2), channel_id=1, source_target_pairs={{0,448},{16,464},{32,480},{48,496},{64,0},{80,16},{96,32},{112,48}... | collective-permute-start | bytes 1376264 | tf_op jit(solution)/shard_map/ppermute | solution.py:10
  381.2 47.5 %collective-permute-start.3 = (bf16[512,448]{1,0:T(8,128)(2,1)S(1)}, bf16[512,448]{1,0:T(8,128)(2,1)}, u32[]{:S(2)}, u32[]{:S(2)}) collective-permute-start(bf16[512,448]{1,0:T(8,128)(2,1)S(1)} %broadcast_select_fusion.5), channel_id=1, source_target_pairs={{0,384},{16,400},{32,416},{48,432},{64,448},{80,464},{96,480},{112... | collective-permute-start | bytes 1376264 | tf_op jit(solution)/shard_map/ppermute | solution.py:10
  404.6 105.3 %collective-permute-start.8 = (bf16[512,448]{1,0:T(8,128)(2,1)S(1)}, bf16[512,448]{1,0:T(8,128)(2,1)}, u32[]{:S(2)}, u32[]{:S(2)}) collective-permute-start(bf16[512,448]{1,0:T(8,128)(2,1)S(1)} %broadcast_select_fusion.4), channel_id=1, source_target_pairs={{0,384},{16,400},{32,416},{48,432},{64,448},{80,464},{96,480},{112... | collective-permute-start | bytes 1376264 | tf_op jit(solution)/shard_map/ppermute | solution.py:10
  428.9 83.1 %collective-permute-start.4 = (bf16[512,448]{1,0:T(8,128)(2,1)S(1)}, bf16[512,448]{1,0:T(8,128)(2,1)}, u32[]{:S(2)}, u32[]{:S(2)}) collective-permute-start(bf16[512,448]{1,0:T(8,128)(2,1)S(1)} %broadcast_select_fusion.7), channel_id=1, source_target_pairs={{0,256},{16,272},{32,288},{48,304},{64,320},{80,336},{96,352},{112... | collective-permute-start | bytes 1376264 | tf_op jit(solution)/shard_map/ppermute | solution.py:10
  510.0 27.0 %collective-permute-start.9 = (bf16[512,448]{1,0:T(8,128)(2,1)S(1)}, bf16[512,448]{1,0:T(8,128)(2,1)}, u32[]{:S(2)}, u32[]{:S(2)}) collective-permute-start(bf16[512,448]{1,0:T(8,128)(2,1)S(1)} %broadcast_select_fusion.6), channel_id=1, source_target_pairs={{0,256},{16,272},{32,288},{48,304},{64,320},{80,336},{96,352},{112... | collective-permute-start | bytes 1376264 | tf_op jit(solution)/shard_map/ppermute | solution.py:10
Sparse Core Ops, SparseCore 0:
  140.7 100.3 reduce-scatter.3
where the time goes:
time: 549 us; the launch traced here: 548 us
  waiting for transfers between devices  234 us (43%)
  blocking collectives  187 us (34%)
  starting transfers between devices  99 us (18%)
  between operations  15 us (3%)
    ppermute x10, waiting for transfers between devices, passed_along(): return lax.ppermute(value, axis, pairs)  134 us
    reduce_scatter x1, waiting for transfers between devices, local(): lax.psum_scatter(jnp.concatenate([gate_term, up_term, grad_term], axis=1)...  101 us
    ppermute x10, starting transfers between devices, passed_along(): return lax.ppermute(value, axis, pairs)  99 us
    all_gather x1, blocking collectives, local(): lax.all_gather(out_grad, 'dp', axis=0, tiled=True)  67.7 us
    all_gather x1, blocking collectives, local(): lax.all_gather(tokens, 'dp', axis=0, tiled=True)  61.8 us
    all_gather x1, blocking collectives, local(): lax.all_gather(grad_share, 'tensor', axis=0, tiled=True)  36.1 us
    all_gather x1, blocking collectives, local(): lax.all_gather(act_share, 'tensor', axis=0, tiled=True)  21.8 us
  transfers between devices with their start and end apart: 11, of which 7 were waited for; matrix products, arithmetic and copies ran while one was open for 1% of the time, Pallas kernels for 0%

commit v1 on v0

v1 whole, which is shorter than its diff:
```python
import jax
import jax.numpy as jnp
from jax import lax
from jax.experimental import pallas as pl
from jax.experimental.pallas import tpu as pltpu
from jax.sharding import PartitionSpec as P

Z, YH, X, YL, CORES = 8, 4, 4, 2, 2
DP, GROUP = Z * YH, X * YL * CORES
CHIPS = X * YL
LEVELS = 32760.0
MESH = pl.DeviceIdType.MESH
f32, bf16, i16, i32 = jnp.float32, jnp.bfloat16, jnp.int16, jnp.int32


def encode(value, largest):
    root = jnp.sqrt(jnp.abs(value)) * (LEVELS * lax.rsqrt(largest))
    code = (root + 0.5).astype(i32)
    return jnp.where(value < 0, -code, code).astype(i16)


def decode(code, unit):
    root = code.astype(i32).astype(f32)
    return root * jnp.abs(root) * unit


def fold(rows):
    half = rows.shape[0] // 2
    return jnp.concatenate([rows[:half], rows[half:]], axis=1)


def unfold(folded):
    width = folded.shape[1] // 2
    return jnp.concatenate([folded[:, :width], folded[:, width:]], axis=0)


def kernel(tok_in, grd_in, wg_in, wu_in, wd_in, pair, act_out, grad_out,
           x_tok, x_grd, wg, wu, wd, pair_tiles, pair_smem,
           ps_act, pr_act, ps_grd, pr_grd, sum_act, sum_grd,
           cs_act, cr_act, cs_grd, cr_grd, us_act, ur_act, us_grd, ur_grd,
           own_act, own_grd, far_act, far_grd, st_act, st_grd, b_act, b_grd,
           tile_act, tile_grd, local_sem, send_sem, recv_sem):
    dp, tensor = lax.axis_index("dp"), lax.axis_index("tensor")
    z, yh = dp // YH, dp % YH
    core, chip = tensor % CORES, tensor // CORES
    x, yl = chip // YL, chip % YL

    def at(dz=0, dyh=0):
        return ((z + dz + Z) % Z * YH + (yh + dyh + YH) % YH, tensor)

    def in_group(dx, dyl, dc, sign=1):
        return (((x + sign * dx + X) % X * YL + (yl + dyl) % YL) * CORES + (core + dc) % CORES)

    used = [0]
    started = []

    def remote(src, dst, device):
        n = used[0]
        used[0] += 1
        return pltpu.make_async_remote_copy(
            src_ref=src, dst_ref=dst, send_sem=send_sem.at[n], recv_sem=recv_sem.at[n],
            device_id=device, device_id_type=MESH)

    def send(src, dst, device):
        copy = remote(src, dst, device)
        copy.start()
        started.append(copy)
        return copy

    peers = [(dx, dyl, dc) for dx in (2, 1, 3, 0) for dyl in (1, 0) for dc in (0, 1) if (dx, dyl, dc) != (0, 0, 0)]
    chip_peers = [(dx, dyl) for dx in (2, 1, 3, 0) for dyl in (1, 0) if (dx, dyl) != (0, 0)]

    loads = [pltpu.make_async_copy(tok_in, x_tok.at[dp], local_sem.at[0]),
             pltpu.make_async_copy(grd_in, x_grd.at[dp], local_sem.at[1]),
             pltpu.make_async_copy(wg_in, wg, local_sem.at[2]),
             pltpu.make_async_copy(wu_in, wu, local_sem.at[3]),
             pltpu.make_async_copy(wd_in, wd, local_sem.at[4])]
    for load in loads:
        load.start()
    barrier = pltpu.get_barrier_semaphore()
    partners = [at(dyh=k) for k in (1, 2, 3)] + [at(dz=1), at(dz=-1)] + [(dp, in_group(*o)) for o in peers]
    for partner in partners:
        pl.semaphore_signal(barrier, inc=1, device_id=partner, device_id_type=MESH)
    distance = (pair[0, 1] - pair[0, 0] + DP) % DP
    pair_tiles[tensor] = jnp.full((8, 128), distance, i32)
    pl.semaphore_wait(barrier, len(partners))

    loads[0].wait()
    loads[1].wait()
    bufs = (x_tok, x_grd)
    from_y = [[None] * YH for _ in bufs]
    ring = {}
    for b, buf in enumerate(bufs):
        for k in (2, 1, 3):
            from_y[b][k] = send(buf.at[dp], buf.at[dp], at(dyh=k))
        for way in (1, -1):
            ring[b, way, 0, 0] = send(buf.at[dp], buf.at[dp], at(dz=way))
    pair_copies = [send(pair_tiles.at[tensor], pair_tiles.at[tensor], (dp, in_group(*o))) for o in peers]
    for k in (1, 3, 2):
        for b, buf in enumerate(bufs):
            from_y[b][k].wait_recv()
            slot = z * YH + (yh - k + YH) % YH
            for way in (1, -1):
                ring[b, way, 0, k] = send(buf.at[slot], buf.at[slot], at(dz=way))
    for hop in (1, 2, 3):
        for b, buf in enumerate(bufs):
            for way in (1, -1):
                for k in range(YH if hop == 1 else 1):
                    ring[b, way, hop - 1, k].wait_recv()
                source = (z - way * hop + Z) % Z * YH
                if hop < 3:
                    rows = pl.ds(source, YH)
                else:
                    rows = pl.ds(source + (0 if way == 1 else YH // 2), YH // 2)
                ring[b, way, hop, 0] = send(buf.at[rows], buf.at[rows], at(dz=way))
    for load in loads[2:]:
        load.wait()

    def rows_of(buf, half):
        return buf[pl.ds(half * (DP // 2), DP // 2)].reshape(buf.shape[1] * DP // 2, buf.shape[2])

    def act_products(half):
        rows = rows_of(x_tok, half)
        return (fold(jnp.dot(rows, wg[...], preferred_element_type=f32)),
                fold(jnp.dot(rows, wu[...], preferred_element_type=f32)))

    def grd_products(half):
        return (fold(lax.dot_general(rows_of(x_grd, half), wd[...], (((1,), (1,)), ((), ())),
                                     preferred_element_type=f32)),)

    other = (dp, in_group(0, 0, 1))
    piece = 16

    def reduce_pair(b, products, ps, pr, total, cs, us):
        for way in (1, -1):
            ring[b, way, 3, 0].wait_recv()
        for i, product in enumerate(products(1 - core)):
            ps[i] = product
        pair = send(ps, pr, other)
        for i, product in enumerate(products(core)):
            total[i] = product
        pair.wait_recv()
        largest = []
        for i in range(total.shape[0]):
            summed = total[i] + pr[i]
            total[i] = summed
            largest.append(jnp.maximum(jnp.max(jnp.abs(summed)), 1e-30))
        for i, most in enumerate(largest):
            us[i] = jnp.full((8, 128), most * (1.0 / (LEVELS * LEVELS)), f32)
            cs[:, i] = encode(total[i], most).reshape(CHIPS, piece, total.shape[2])

    def spread(cs, cr, us, ur):
        copies = []
        for n, (dx, dyl) in enumerate(chip_peers):
            there = in_group(dx, dyl, 0)
            copies.append((send(us, ur.at[n], (dp, there)),
                           send(cs.at[there // CORES], cr.at[n], (dp, there))))
        return copies

    def gathered(copies, total, cr, ur):
        mine = [total[i, pl.ds(chip * piece, piece)] for i in range(total.shape[0])]
        for n, copy in enumerate(copies):
            for c in copy:
                c.wait_recv()
            for i in range(total.shape[0]):
                mine[i] += decode(cr[n, i], ur[n, i, 0:1, 0:1])
        return mine

    reduce_pair(0, act_products, ps_act, pr_act, sum_act, cs_act, us_act)
    c_act = spread(cs_act, cr_act, us_act, ur_act)
    reduce_pair(1, grd_products, ps_grd, pr_grd, sum_grd, cs_grd, us_grd)
    c_grd = spread(cs_grd, cr_grd, us_grd, ur_grd)

    def share_out(own):
        first = [send(own.at[tensor], own.at[tensor], (dp, in_group(dx, dyl, 0))) for dx, dyl in chip_peers]
        return first, [send(own.at[tensor], own.at[tensor], other)]

    def pass_on(own, first, second):
        for (dx, dyl), copy in zip(chip_peers, first):
            copy.wait_recv()
            slot = in_group(dx, dyl, 0, sign=-1)
            second.append(send(own.at[slot], own.at[slot], other))

    gate, up = gathered(c_act, sum_act, cr_act, ur_act)
    hidden = (gate / (1.0 + jnp.exp(-gate)) * up).astype(bf16)
    own_act[tensor] = hidden
    far_act[yh] = hidden
    act_y = {k: send(far_act.at[yh], far_act.at[yh], at(dyh=k)) for k in (2, 1, 3)}
    act_z = {(0, 0): send(far_act.at[yh], far_act.at[YH + yh], at(dz=-1))}
    d_act = share_out(own_act)

    (grad_sum,) = gathered(c_grd, sum_grd, cr_grd, ur_grd)
    hidden_grad = grad_sum.astype(bf16)
    own_grd[tensor] = hidden_grad
    far_grd[yh] = hidden_grad
    grd_z = [send(far_grd.at[yh], far_grd.at[YH + yh], at(dz=-1))]
    d_grd = share_out(own_grd)

    for k in (1, 3, 2):
        act_y[k].wait_recv()
        slot = (yh - k + YH) % YH
        act_z[0, k] = send(far_act.at[slot], far_act.at[YH + slot], at(dz=-1))

    grd_y = {}
    for k in (2, 1, 3):
        grd_y[0, k] = remote(far_grd.at[yh], far_grd.at[yh], at(dyh=k))
        pl.when((yh + k) % YH < yh)(grd_y[0, k].start)
    for hop in (1, 2, 3, 4):
        slot = hop * YH + yh
        grd_z[hop - 1].wait_recv()
        if hop < 4:
            grd_z.append(send(far_grd.at[slot], far_grd.at[slot + YH], at(dz=-1)))
        for k in (2, 1, 3):
            grd_y[hop, k] = remote(far_grd.at[slot], far_grd.at[slot], at(dyh=k))
            if hop < 4:
                grd_y[hop, k].start()
                started.append(grd_y[hop, k])
            else:
                pl.when((yh + k) % YH > yh)(grd_y[hop, k].start)
        if hop < 4:
            for k in range(YH):
                there = (yh - k + YH) % YH
                act_z[hop - 1, k].wait_recv()
                row = hop * YH + there
                act_z[hop, k] = remote(far_act.at[row], far_act.at[row + YH], at(dz=-1))
                if hop < 3:
                    act_z[hop, k].start()
                    started.append(act_z[hop, k])
                else:
                    pl.when(there <= yh)(act_z[hop, k].start)
        if hop == 1:
            pass_on(own_act, *d_act)
        if hop == 2:
            pass_on(own_grd, *d_grd)

    for copy in pair_copies:
        copy.wait_recv()
    to_smem = pltpu.make_async_copy(pair_tiles, pair_smem, local_sem.at[0])
    to_smem.start()
    to_smem.wait()

    def deliver(far, st, b):
        for j in range(GROUP):
            st[j] = far[yh + pair_smem[j, 0, 0]]
        copies = [send(st.at[in_group(*o)], b.at[tensor], (dp, in_group(*o))) for o in peers]
        b[tensor] = st[tensor]
        return copies

    for k in range(YH):
        there = (yh - k + YH) % YH
        pl.when(there <= yh)(act_z[3, k].wait_recv)
    e_act = deliver(far_act, st_act, b_act)
    for k in (1, 2, 3):
        there = (yh - k + YH) % YH
        pl.when(yh < there)(grd_y[0, k].wait_recv)
        for hop in (1, 2, 3):
            grd_y[hop, k].wait_recv()
        pl.when(yh > there)(grd_y[4, k].wait_recv)
    e_grd = deliver(far_grd, st_grd, b_grd)

    diagonal = (distance == DP // 2) & (dp >= DP // 2)
    is_diagonal = jnp.full((1, 1), jnp.where(diagonal, 1, 0), i32) == 1

    def tile(own, b, second, delivered, out, sem):
        for copy in second:
            copy.wait_recv()
        for copy in delivered:
            copy.wait_recv()
        left = unfold(own[...].reshape(GROUP * piece, own.shape[2]))
        far = unfold(b[...].reshape(GROUP * piece, b.shape[2]))
        right = jnp.where(jnp.broadcast_to(is_diagonal, far.shape), left, far)
        dims = (((0,), (0,)), ((), ()))
        upper = lax.dot_general(left, right, dims, preferred_element_type=f32)
        lower = lax.dot_general(far, far, dims, preferred_element_type=f32)
        p = lax.broadcasted_iota(i32, upper.shape, 0)
        q = lax.broadcasted_iota(i32, upper.shape, 1)
        take_lower = jnp.where(p > q, jnp.where(is_diagonal, 1, 0), 0) == 1
        sem[...] = jnp.where(take_lower, lower, upper) * (1.0 / (DP * 16))

    tile(own_act, b_act, d_act[1], e_act, None, tile_act)
    write_act = pltpu.make_async_copy(tile_act, act_out.at[0], local_sem.at[1])
    write_act.start()
    tile(own_grd, b_grd, d_grd[1], e_grd, None, tile_grd)
    write_grd = pltpu.make_async_copy(tile_grd, grad_out.at[0], local_sem.at[2])
    write_grd.start()

    for copy in started:
        copy.wait_send()
    for k in (1, 2, 3):
        pl.when((yh + k) % YH < yh)(grd_y[0, k].wait_send)
        pl.when((yh + k) % YH > yh)(grd_y[4, k].wait_send)
    for k in range(YH):
        pl.when((yh - k + YH) % YH <= yh)(act_z[3, k].wait_send)
    write_act.wait()
    write_grd.wait()


def local(tokens, out_grad, gate_weight, up_weight, down_weight, pair_list):
    rows, depth = tokens.shape
    width = gate_weight.shape[1]
    half = rows * DP // 4
    piece = half // CHIPS
    any_space = pl.BlockSpec(memory_space=pl.ANY)
    tile = jax.ShapeDtypeStruct((1, width, width), f32)

    def vmem(shape, kind):
        return pltpu.VMEM(shape, kind)

    scratch = [
        vmem((DP, rows, depth), bf16), vmem((DP, rows, depth), bf16),
        vmem((depth, width), bf16), vmem((depth, width), bf16), vmem((width, depth), bf16),
        vmem((GROUP, 8, 128), i32), pltpu.SMEM((GROUP, 8, 128), i32),
        vmem((2, half, 2 * width), f32), vmem((2, half, 2 * width), f32),
        vmem((1, half, 2 * width), f32), vmem((1, half, 2 * width), f32),
        vmem((2, half, 2 * width), f32), vmem((1, half, 2 * width), f32),
        vmem((CHIPS, 2, piece, 2 * width), i16), vmem((CHIPS - 1, 2, piece, 2 * width), i16),
        vmem((CHIPS, 1, piece, 2 * width), i16), vmem((CHIPS - 1, 1, piece, 2 * width), i16),
        vmem((2, 8, 128), f32), vmem((CHIPS - 1, 2, 8, 128), f32),
        vmem((1, 8, 128), f32), vmem((CHIPS - 1, 1, 8, 128), f32),
        vmem((GROUP, piece, 2 * width), bf16), vmem((GROUP, piece, 2 * width), bf16),
        vmem((5 * YH, piece, 2 * width), bf16), vmem((5 * YH, piece, 2 * width), bf16),
        vmem((GROUP, piece, 2 * width), bf16), vmem((GROUP, piece, 2 * width), bf16),
        vmem((GROUP, piece, 2 * width), bf16), vmem((GROUP, piece, 2 * width), bf16),
        vmem((width, width), f32), vmem((width, width), f32),
        pltpu.SemaphoreType.DMA((5,)), pltpu.SemaphoreType.DMA((200,)), pltpu.SemaphoreType.DMA((200,)),
    ]
    return pl.pallas_call(
        kernel,
        out_shape=(tile, tile),
        in_specs=[any_space] * 5 + [pl.BlockSpec(memory_space=pltpu.SMEM)],
        out_specs=(any_space, any_space),
        scratch_shapes=scratch,
        compiler_params=pltpu.CompilerParams(
            collective_id=0, has_side_effects=True, vmem_limit_bytes=48 * 1024 * 1024),
        name="covariance",
    )(tokens, out_grad, gate_weight, up_weight, down_weight, pair_list)


def solution(mesh):
    in_specs = (
        P("dp", "tensor"),
        P("dp", "tensor"),
        P("tensor", "dp"),
        P("tensor", "dp"),
        P("dp", "tensor"),
        P(("dp", "tensor"), None),
    )
    out_specs = (P(("dp", "tensor"), None, None), P(("dp", "tensor"), None, None))
    return jax.shard_map(local, mesh=mesh, in_specs=in_specs, out_specs=out_specs, check_vma=False)
```

time: 549 us -> 86.2 us (0.16)
  the two profiles are of different devices: /device:TPU:177 before, /device:TPU:1 now
where the time goes in v1:
time: 86.2 us; the launch traced here: 86.1 us
  Pallas kernels  81.2 us (94%)
  local copies, waits for them, and re-layouts  4.12 us (5%)
    pallas_call x1, Pallas kernels, local(): pl.pallas_call(kernel, out_shape=(tile, tile), in_specs=[any_space] * 5 +...  81.2 us
    unnamed x14, local copies, waits for them, and re-layouts  4.12 us

profile of v1, /device:TPU:1, one launch (start us, length us, event | category | flops | bytes accessed | tf_op | source)
XLA Modules:
  0.0 86.1 jit_solution(12135236119997425406)
XLA Ops:
  0.6 0.0 copy-start.4
  0.6 1.3 %copy.8.wg_in = bf16[512,448]{1,0:T(8,128)(2,1)S(1)} copy(bf16[512,448]{0,1:T(8,128)(2,1)} %param.8) | data formatting | bytes 917504 | tf_op args[2]
  1.9 0.0 copy-done.4
  1.9 0.0 copy-start
  1.9 0.0 copy-start.1
  2.0 0.0 copy-start.2
  2.0 0.0 copy-start.3
  2.0 0.2 copy.9.wu_in
  2.2 0.8 copy-done
  3.0 0.0 copy-done.1
  3.0 0.0 copy-done.2
  3.0 0.0 copy-done.3
  3.0 81.2 %covariance.1 = (f32[1,448,448]{2,1,0:T(8,128)S(1)}, f32[1,448,448]{2,1,0:T(8,128)S(1)}) custom-call(bf16[16,512]{1,0:T(8,128)(2,1)S(1)} %copy-done.1, bf16[16,512]{1,0:T(8,128)(2,1)S(1)} %copy-done.2, bf16[512,448]{1,0:T(8,128)(2,1)S(1)} %copy.8.wg_in, bf16[512,448]{1,0:T(8,128)(2,1)S(1)} %copy.9.wu_in, bf16[448,512]{1,0:T(8,128)(2,1)S(1)} %copy-done, ...), custom_call_target="tpu_custom_call" | custom-call | tf_op jit(solution)/shard_map/covariance/pallas_call | solution.py:327
  84.2 0.9 %copy.12 = f32[1,448,448]{2,1,0:T(8,128)} copy(f32[1,448,448]{2,1,0:T(8,128)S(1)} %get-tuple-element.4) | data formatting | bytes 1605632
  85.1 0.9 %copy.13 = f32[1,448,448]{2,1,0:T(8,128)} copy(f32[1,448,448]{2,1,0:T(8,128)S(1)} %get-tuple-element.5) | data formatting | bytes 1605632
Async XLA Ops:
  0.6 1.3 %copy-start.4 = (bf16[512,448]{0,1:T(8,128)(2,1)S(1)}, bf16[512,448]{0,1:T(8,128)(2,1)}, u32[]{:S(2)}) copy-start(bf16[512,448]{0,1:T(8,128)(2,1)} %param.9) | copy-start | bytes 1376260
  1.9 1.0 %copy-start = (bf16[448,512]{1,0:T(8,128)(2,1)S(1)}, bf16[448,512]{1,0:T(8,128)(2,1)}, u32[]{:S(2)}) copy-start(bf16[448,512]{1,0:T(8,128)(2,1)} %wd_in.1) | copy-start | bytes 1376260
  1.9 1.0 %copy-start.1 = (bf16[16,512]{1,0:T(8,128)(2,1)S(1)}, bf16[16,512]{1,0:T(8,128)(2,1)}, u32[]{:S(2)}) copy-start(bf16[16,512]{1,0:T(8,128)(2,1)} %tok_in.1) | copy-start | bytes 49156
  2.0 1.0 %copy-start.2 = (bf16[16,512]{1,0:T(8,128)(2,1)S(1)}, bf16[16,512]{1,0:T(8,128)(2,1)}, u32[]{:S(2)}) copy-start(bf16[16,512]{1,0:T(8,128)(2,1)} %grd_in.1) | copy-start | bytes 49156
  2.0 1.0 %copy-start.3 = (s32[1,2]{1,0:T(1,128)S(1)}, s32[1,2]{1,0:T(1,128)}, u32[]{:S(2)}) copy-start(s32[1,2]{1,0:T(1,128)} %pair.1) | copy-start | bytes 28

commit v2 on v1

v2 whole, which is shorter than its diff:
```python
import jax
import jax.numpy as jnp
from jax import lax
from jax.experimental import pallas as pl
from jax.experimental.pallas import tpu as pltpu
from jax.sharding import PartitionSpec as P

Z, YH, X, YL, CORES = 8, 4, 4, 2, 2
DP, GROUP = Z * YH, X * YL * CORES
CHIPS = X * YL
LEVELS = 32760.0
MESH = pl.DeviceIdType.MESH
f32, bf16, i16, i32 = jnp.float32, jnp.bfloat16, jnp.int16, jnp.int32


def encode(value, largest):
    root = jnp.sqrt(jnp.abs(value)) * (LEVELS * lax.rsqrt(largest))
    code = (root + 0.5).astype(i32)
    return jnp.where(value < 0, -code, code).astype(i16)


def decode(code, unit):
    root = code.astype(i32).astype(f32)
    return root * jnp.abs(root) * unit


def fold(rows):
    half = rows.shape[0] // 2
    return jnp.concatenate([rows[:half], rows[half:]], axis=1)


def unfold(folded):
    width = folded.shape[1] // 2
    return jnp.concatenate([folded[:, :width], folded[:, width:]], axis=0)


def kernel(tok_in, grd_in, wg_in, wu_in, wd_in, pair, act_out, grad_out,
           x_tok, x_grd, wg, wu, wd, pair_tiles, pair_smem,
           ps_act, pr_act, ps_grd, pr_grd, sum_act, sum_grd,
           cs_act, cr_act, cs_grd, cr_grd, us_act, ur_act, us_grd, ur_grd,
           own_act, own_grd, far_act, far_grd, pass_act, pass_grd, st_act, st_grd, b_act, b_grd,
           tile_act, tile_grd, local_sem, send_sem, recv_sem):
    dp, tensor = lax.axis_index("dp"), lax.axis_index("tensor")
    z, yh = dp // YH, dp % YH
    core, chip = tensor % CORES, tensor // CORES
    x, yl = chip // YL, chip % YL

    def at(dz=0, dyh=0):
        return ((z + dz + Z) % Z * YH + (yh + dyh + YH) % YH, tensor)

    def in_group(dx, dyl, dc, sign=1):
        return (((x + sign * dx + X) % X * YL + (yl + dyl) % YL) * CORES + (core + dc) % CORES)

    used = [0]
    sent = []

    def send(src, dst, device, only=None):
        n = used[0]
        used[0] += 1
        copy = pltpu.make_async_remote_copy(
            src_ref=src, dst_ref=dst, send_sem=send_sem.at[n], recv_sem=recv_sem.at[n],
            device_id=device, device_id_type=MESH)
        if only is None:
            copy.start()
        else:
            pl.when(only)(copy.start)
        sent.append((only, copy))
        return copy

    peers = [(dx, dyl, dc) for dx in (2, 1, 3, 0) for dyl in (1, 0) for dc in (0, 1) if (dx, dyl, dc) != (0, 0, 0)]
    chip_peers = [(dx, dyl) for dx in (2, 1, 3, 0) for dyl in (1, 0) if (dx, dyl) != (0, 0)]

    barrier = pltpu.get_barrier_semaphore()
    partners = [at(dyh=k) for k in (1, 2, 3)] + [at(dz=k) for k in (1, -1, 2, -2)] + [(dp, in_group(*o)) for o in peers]
    for partner in partners:
        pl.semaphore_signal(barrier, inc=1, device_id=partner, device_id_type=MESH)
    loads = [pltpu.make_async_copy(tok_in, x_tok.at[dp], local_sem.at[0]),
             pltpu.make_async_copy(grd_in, x_grd.at[dp], local_sem.at[1]),
             pltpu.make_async_copy(wg_in, wg, local_sem.at[2]),
             pltpu.make_async_copy(wu_in, wu, local_sem.at[3]),
             pltpu.make_async_copy(wd_in, wd, local_sem.at[4])]
    for load in loads:
        load.start()
    distance = (pair[0, 1] - pair[0, 0] + DP) % DP
    pair_tiles[tensor] = jnp.full((8, 128), distance, i32)
    pl.semaphore_wait(barrier, len(partners))

    def y_slot(k):
        return (yh - k + YH) % YH

    ring = {}

    def along_z(b, buf, src, k):
        slot = z * YH + y_slot(k)
        for step in (2, 1):
            for way in (1, -1):
                ring[b, way, step, k] = send(src, buf.at[slot], at(dz=way * step))

    def pass_along_z(b, buf, k):
        for way in (1, -1):
            ring[b, way, 2, k].wait_recv()
            slot = (z - way * 2 + Z) % Z * YH + y_slot(k)
            if (way == 1) == (k in (0, 2)):
                ring[b, way, 4, k] = send(buf.at[slot], buf.at[slot], at(dz=way * 2))
            ring[b, way, 3, k] = send(buf.at[slot], buf.at[slot], at(dz=way))

    def all_rows(b, pieces):
        for k in pieces:
            for way in (1, -1):
                if b == 1 or k != 0:
                    ring[b, way, 1, k].wait_recv()
                    ring[b, way, 3, k].wait_recv()
                    if (b, way, 4, k) in ring:
                        ring[b, way, 4, k].wait_recv()

    y_tok = {}
    y_tok[0, 2] = send(tok_in, x_tok.at[dp], at(dyh=2))
    along_z(0, x_tok, tok_in, 0)
    for k in (1, 3):
        y_tok[0, k] = send(tok_in, x_tok.at[dp], at(dyh=k))
    y_grd = {k: send(grd_in, x_grd.at[dp], at(dyh=k)) for k in (2, 1, 3)}

    def to_neighbours(shift):
        slot = (z - shift + Z) % Z * YH + yh
        for k in (1, 3):
            y_tok[shift, k] = send(x_tok.at[slot], x_tok.at[slot], at(dyh=k))

    for way in (1, -1):
        ring[0, way, 1, 0].wait_recv()
        to_neighbours(way)
    pass_along_z(0, x_tok, 0)
    to_neighbours(2)
    to_neighbours(-2)
    y_tok[0, 2].wait_recv()
    along_z(0, x_tok, x_tok.at[z * YH + y_slot(2)], 2)
    along_z(1, x_grd, grd_in, 0)
    for way in (1, -1):
        ring[0, way, 3, 0].wait_recv()
        to_neighbours(way * 3)
    ring[0, 1, 4, 0].wait_recv()
    to_neighbours(4)
    pass_along_z(0, x_tok, 2)
    for k in (1, 3, 2):
        y_grd[k].wait_recv()
        along_z(1, x_grd, x_grd.at[z * YH + y_slot(k)], k)
    pair_copies = [send(pair_tiles.at[tensor], pair_tiles.at[tensor], (dp, in_group(*o))) for o in peers]
    for load in loads:
        load.wait()

    other = (dp, in_group(0, 0, 1))
    piece = cs_act.shape[2]

    def product(buf, half, weight):
        rows = buf[pl.ds(half * (DP // 2), DP // 2)].reshape(buf.shape[1] * DP // 2, buf.shape[2])
        return fold(lax.dot_general(rows, weight[...], (((1,), (1,)), ((), ())), preferred_element_type=f32))

    def for_other(buf, weights, ps, pr):
        pairs = []
        for i, weight in enumerate(weights):
            ps[i] = product(buf, 1 - core, weight)
            pairs.append(send(ps.at[i], pr.at[i], other))
        return pairs

    def rows_of_chip(q):
        return pl.ds(pl.multiple_of(q * piece, piece), piece)

    def spread(pairs, total, pr, cs, us, cr, ur):
        for pair_copy in pairs:
            pair_copy.wait_recv()
        copies = []
        for n, (dx, dyl) in enumerate(chip_peers):
            there = in_group(dx, dyl, 0)
            q = there // CORES
            for i in range(total.shape[0]):
                summed = total[i, rows_of_chip(q)] + pr[i, rows_of_chip(q)]
                most = jnp.maximum(jnp.max(jnp.abs(summed)), 1e-30)
                us[q, i] = jnp.full((8, 128), most * (1.0 / (LEVELS * LEVELS)), f32)
                cs[q, i] = encode(summed, most)
            copies.append((send(us.at[q], ur.at[n], (dp, there)), send(cs.at[q], cr.at[n], (dp, there))))
        return copies

    def gathered(copies, total, pr, cr, ur):
        mine = [total[i, rows_of_chip(chip)] + pr[i, rows_of_chip(chip)] for i in range(total.shape[0])]
        for n, copy in enumerate(copies):
            for c in copy:
                c.wait_recv()
            for i in range(total.shape[0]):
                mine[i] += decode(cr[n, i], ur[n, i, 0:1, 0:1])
        return mine

    all_rows(0, (2,))
    for shift in (0, 1, -1, 2, -2, 3, -3, 4):
        for k in (1, 3):
            y_tok[shift, k].wait_recv()
    pairs = for_other(x_tok, (wg, wu), ps_act, pr_act)
    for k in (0, 1, 3, 2):
        pass_along_z(1, x_grd, k)
    for i, weight in enumerate((wg, wu)):
        sum_act[i] = product(x_tok, core, weight)
    c_act = spread(pairs, sum_act, pr_act, cs_act, us_act, cr_act, ur_act)
    all_rows(1, range(YH))
    pairs = for_other(x_grd, (wd,), ps_grd, pr_grd)
    sum_grd[0] = product(x_grd, core, wd)
    c_grd = spread(pairs, sum_grd, pr_grd, cs_grd, us_grd, cr_grd, ur_grd)

    for copy in pair_copies:
        copy.wait_recv()
    to_smem = pltpu.make_async_copy(pair_tiles, pair_smem, local_sem.at[0])
    to_smem.start()
    to_smem.wait()

    far_x = (2, 1, 3)

    def share_out(own):
        across = send(own.at[tensor], own.at[tensor], (dp, in_group(0, 1, 0)))
        along = [send(own.at[tensor], own.at[tensor], (dp, in_group(dx, 0, 0))) for dx in far_x]
        return across, along, [send(own.at[tensor], own.at[tensor], other)]

    def pass_across(own, across, along, second):
        across.wait_recv()
        slot = in_group(0, 1, 0)
        along += [send(own.at[slot], own.at[slot], (dp, in_group(dx, 0, 0))) for dx in far_x]
        second.append(send(own.at[slot], own.at[slot], other))

    def pass_on(own, across, along, second):
        for n, copy in enumerate(along):
            copy.wait_recv()
            slot = in_group(far_x[n % 3], n // 3, 0, sign=-1)
            second.append(send(own.at[slot], own.at[slot], other))

    def down_z(far, through, k, e_z):
        slot = y_slot(k)
        e_z[2, k] = send(far.at[slot], far.at[2 * YH + slot], at(dz=-2))
        e_z[-2, k] = send(far.at[slot], through.at[slot], at(dz=2), None if k == 0 else slot <= yh)
        e_z[1, k] = send(far.at[slot], far.at[YH + slot], at(dz=-1))

    def pass_down_z(far, through, k, e_z):
        slot = y_slot(k)
        e_z[2, k].wait_recv()
        e_z[3, k] = send(far.at[2 * YH + slot], far.at[3 * YH + slot], at(dz=-1))
        if k == 0:
            e_z[-2, k].wait_recv()
            e_z[4, k] = send(through.at[slot], far.at[4 * YH + slot], at(dz=2))
        else:
            pl.when(slot <= yh)(e_z[-2, k].wait_recv)
            e_z[4, k] = send(through.at[slot], far.at[4 * YH + slot], at(dz=2), slot <= yh)

    gate, up = gathered(c_act, sum_act, pr_act, cr_act, ur_act)
    hidden = (gate / (1.0 + jnp.exp(-gate)) * up).astype(bf16)
    own_act[tensor] = hidden
    far_act[yh] = hidden
    act_y = {k: send(far_act.at[yh], far_act.at[yh], at(dyh=k)) for k in (2, 1, 3)}
    act_z = {}
    down_z(far_act, pass_act, 0, act_z)
    d_act = share_out(own_act)

    (grad_sum,) = gathered(c_grd, sum_grd, pr_grd, cr_grd, ur_grd)
    hidden_grad = grad_sum.astype(bf16)
    own_grd[tensor] = hidden_grad
    far_grd[yh] = hidden_grad
    grd_z, grd_y = {}, {}
    down_z(far_grd, pass_grd, 0, grd_z)
    for k in (2, 1, 3):
        grd_y[0, k] = send(far_grd.at[yh], far_grd.at[yh], at(dyh=k), (yh + k) % YH < yh)
    d_grd = share_out(own_grd)

    def over_y(hop):
        slot = hop * YH + yh
        for k in (2, 1, 3):
            grd_y[hop, k] = send(far_grd.at[slot], far_grd.at[slot], at(dyh=k), None if hop < 4 else (yh + k) % YH > yh)

    pass_down_z(far_act, pass_act, 0, act_z)
    for k in (1, 3, 2):
        act_y[k].wait_recv()
        down_z(far_act, pass_act, k, act_z)
    grd_z[1, 0].wait_recv()
    over_y(1)
    pass_down_z(far_grd, pass_grd, 0, grd_z)
    over_y(2)
    pass_across(own_act, *d_act)
    pass_across(own_grd, *d_grd)
    for k in (1, 3, 2):
        pass_down_z(far_act, pass_act, k, act_z)
    for hop in (3, 4):
        grd_z[hop, 0].wait_recv()
        over_y(hop)
    pass_on(own_act, *d_act)
    pass_on(own_grd, *d_grd)

    def deliver(far, st, b):
        for j in range(GROUP):
            st[j] = far[yh + pair_smem[j, 0, 0]]
        copies = [send(st.at[in_group(*o)], b.at[tensor], (dp, in_group(*o))) for o in peers]
        b[tensor] = st[tensor]
        return copies

    for k in range(YH):
        act_z[1, k].wait_recv()
        act_z[3, k].wait_recv()
        if k == 0:
            act_z[4, k].wait_recv()
        else:
            pl.when(y_slot(k) <= yh)(act_z[4, k].wait_recv)
    e_act = deliver(far_act, st_act, b_act)
    for k in (1, 2, 3):
        there = y_slot(k)
        pl.when(yh < there)(grd_y[0, k].wait_recv)
        for hop in (1, 2, 3):
            grd_y[hop, k].wait_recv()
        pl.when(yh > there)(grd_y[4, k].wait_recv)
    e_grd = deliver(far_grd, st_grd, b_grd)

    diagonal = (distance == DP // 2) & (dp >= DP // 2)
    is_diagonal = jnp.full((1, 1), jnp.where(diagonal, 1, 0), i32) == 1

    def tile(own, b, second, delivered, out):
        for copy in second + delivered:
            copy.wait_recv()
        left = unfold(own[...].reshape(GROUP * piece, own.shape[2]))
        far = unfold(b[...].reshape(GROUP * piece, b.shape[2]))
        right = jnp.where(jnp.broadcast_to(is_diagonal, far.shape), left, far)
        dims = (((0,), (0,)), ((), ()))
        upper = lax.dot_general(left, right, dims, preferred_element_type=f32)
        lower = lax.dot_general(far, far, dims, preferred_element_type=f32)
        p = lax.broadcasted_iota(i32, upper.shape, 0)
        q = lax.broadcasted_iota(i32, upper.shape, 1)
        take_lower = jnp.where(p > q, jnp.where(is_diagonal, 1, 0), 0) == 1
        out[...] = jnp.where(take_lower, lower, upper) * (1.0 / (DP * 16))

    tile(own_act, b_act, d_act[2], e_act, tile_act)
    write_act = pltpu.make_async_copy(tile_act, act_out.at[0], local_sem.at[1])
    write_act.start()
    tile(own_grd, b_grd, d_grd[2], e_grd, tile_grd)
    write_grd = pltpu.make_async_copy(tile_grd, grad_out.at[0], local_sem.at[2])
    write_grd.start()

    for only, copy in sent:
        if only is None:
            copy.wait_send()
        else:
            pl.when(only)(copy.wait_send)
    write_act.wait()
    write_grd.wait()


def local(tokens, out_grad, gate_weight, up_weight, down_weight, pair_list):
    rows, depth = tokens.shape
    width = gate_weight.shape[1]
    half = rows * DP // 4
    piece = half // CHIPS
    any_space = pl.BlockSpec(memory_space=pl.ANY)
    tile = jax.ShapeDtypeStruct((1, width, width), f32)

    def vmem(shape, kind):
        return pltpu.VMEM(shape, kind)

    scratch = [
        vmem((DP, rows, depth), bf16), vmem((DP, rows, depth), bf16),
        vmem((width, depth), bf16), vmem((width, depth), bf16), vmem((width, depth), bf16),
        vmem((GROUP, 8, 128), i32), pltpu.SMEM((GROUP, 8, 128), i32),
        vmem((2, half, 2 * width), f32), vmem((2, half, 2 * width), f32),
        vmem((1, half, 2 * width), f32), vmem((1, half, 2 * width), f32),
        vmem((2, half, 2 * width), f32), vmem((1, half, 2 * width), f32),
        vmem((CHIPS, 2, piece, 2 * width), i16), vmem((CHIPS - 1, 2, piece, 2 * width), i16),
        vmem((CHIPS, 1, piece, 2 * width), i16), vmem((CHIPS - 1, 1, piece, 2 * width), i16),
        vmem((CHIPS, 2, 8, 128), f32), vmem((CHIPS - 1, 2, 8, 128), f32),
        vmem((CHIPS, 1, 8, 128), f32), vmem((CHIPS - 1, 1, 8, 128), f32),
        vmem((GROUP, piece, 2 * width), bf16), vmem((GROUP, piece, 2 * width), bf16),
        vmem((5 * YH, piece, 2 * width), bf16), vmem((5 * YH, piece, 2 * width), bf16),
        vmem((YH, piece, 2 * width), bf16), vmem((YH, piece, 2 * width), bf16),
        vmem((GROUP, piece, 2 * width), bf16), vmem((GROUP, piece, 2 * width), bf16),
        vmem((GROUP, piece, 2 * width), bf16), vmem((GROUP, piece, 2 * width), bf16),
        vmem((width, width), f32), vmem((width, width), f32),
        pltpu.SemaphoreType.DMA((5,)), pltpu.SemaphoreType.DMA((256,)), pltpu.SemaphoreType.DMA((256,)),
    ]
    return pl.pallas_call(
        kernel,
        out_shape=(tile, tile),
        in_specs=[any_space] * 5 + [pl.BlockSpec(memory_space=pltpu.SMEM)],
        out_specs=(any_space, any_space),
        scratch_shapes=scratch,
        compiler_params=pltpu.CompilerParams(
            collective_id=0, has_side_effects=True, vmem_limit_bytes=60 * 1024 * 1024),
        name="covariance",
    )(tokens, out_grad, gate_weight.T, up_weight.T, down_weight, pair_list)


def solution(mesh):
    in_specs = (
        P("dp", "tensor"),
        P("dp", "tensor"),
        P("tensor", "dp"),
        P("tensor", "dp"),
        P("dp", "tensor"),
        P(("dp", "tensor"), None),
    )
    out_specs = (P(("dp", "tensor"), None, None), P(("dp", "tensor"), None, None))
    return jax.shard_map(local, mesh=mesh, in_specs=in_specs, out_specs=out_specs, check_vma=False)
```

time: 86.2 us -> 79.5 us (0.922)
  Pallas kernels: 81.2 us -> 75.5 us
  local copies, waits for them, and re-layouts: 4.12 us -> 3.17 us
    pallas_call x1, Pallas kernels: 81.2 us -> 75.5 us  [local(): pl.pallas_call(kernel, out_shape=(tile, tile), in_specs=[any_space] * 5 +...]
    unnamed x14 -> x4, local copies, waits for them, and re-layouts: 4.12 us -> 3.17 us
where the time goes in v2:
time: 79.5 us; the launch traced here: 79.3 us
  Pallas kernels  75.5 us (95%)
  local copies, waits for them, and re-layouts  3.17 us (4%)
    pallas_call x1, Pallas kernels, local(): pl.pallas_call(kernel, out_shape=(tile, tile), in_specs=[any_space] * 5 +...  75.5 us
    unnamed x4, local copies, waits for them, and re-layouts  3.17 us

profile of v2, /device:TPU:1, one launch (start us, length us, event | category | flops | bytes accessed | tf_op | source)
XLA Modules:
  0.0 79.3 jit_solution(6336211191546072227)
XLA Ops:
  0.6 75.5 %covariance.1 = (f32[1,448,448]{2,1,0:T(8,128)}, f32[1,448,448]{2,1,0:T(8,128)}) custom-call(bf16[16,512]{1,0:T(8,128)(2,1)} %tok_in.1, bf16[16,512]{1,0:T(8,128)(2,1)} %grd_in.1, bf16[448,512]{1,0:T(8,128)(2,1)} %bitcast.2, bf16[448,512]{1,0:T(8,128)(2,1)} %bitcast.3, bf16[448,512]{1,0:T(8,128)(2,1)} %wd_in.1, s32[1,2]{1,0:T(1,128)} %pair.1), custom_call_target="tpu_custom_call" | custom-call | tf_op jit(solution)/shard_map/covariance/pallas_call | solution.py:376
  76.1 0.0 copy-start
  76.1 2.2 %copy.10 = f32[1,448,448]{2,1,0:T(8,128)} copy(f32[1,448,448]{2,1,0:T(8,128)} %get-tuple-element.4) | data formatting | bytes 1605632
  78.4 0.0 copy-done
  78.4 0.9 %copy.11 = f32[1,448,448]{2,1,0:T(8,128)} copy(f32[1,448,448]{2,1,0:T(8,128)S(1)} %copy-done) | data formatting | bytes 1605632
Async XLA Ops:
  76.1 2.3 %copy-start = (f32[1,448,448]{2,1,0:T(8,128)S(1)}, f32[1,448,448]{2,1,0:T(8,128)}, u32[]{:S(2)}) copy-start(f32[1,448,448]{2,1,0:T(8,128)} %get-tuple-element.5) | copy-start | bytes 2408452

commit v3 on v2

--- a/solution.py
+++ b/solution.py
@@ -38,7 +38,7 @@
            x_tok, x_grd, wg, wu, wd, pair_tiles, pair_smem,
            ps_act, pr_act, ps_grd, pr_grd, sum_act, sum_grd,
            cs_act, cr_act, cs_grd, cr_grd, us_act, ur_act, us_grd, ur_grd,
-           own_act, own_grd, far_act, far_grd, pass_act, pass_grd, st_act, st_grd, b_act, b_grd,
+           own_act, own_grd, far_act, far_grd, pass_grd, st_act, st_grd, b_act, b_grd,
            tile_act, tile_grd, local_sem, send_sem, recv_sem):
     dp, tensor = lax.axis_index("dp"), lax.axis_index("tensor")
     z, yh = dp // YH, dp % YH
@@ -71,7 +71,7 @@
     chip_peers = [(dx, dyl) for dx in (2, 1, 3, 0) for dyl in (1, 0) if (dx, dyl) != (0, 0)]
 
     barrier = pltpu.get_barrier_semaphore()
-    partners = [at(dyh=k) for k in (1, 2, 3)] + [at(dz=k) for k in (1, -1, 2, -2)] + [(dp, in_group(*o)) for o in peers]
+    partners = [at(dyh=k) for k in (1, 2, 3)] + [at(dz=k) for k in (1, -1, 2, -2, 3, -3, 4)] + [(dp, in_group(*o)) for o in peers]
     for partner in partners:
         pl.semaphore_signal(barrier, inc=1, device_id=partner, device_id_type=MESH)
     loads = [pltpu.make_async_copy(tok_in, x_tok.at[dp], local_sem.at[0]),
@@ -104,18 +104,25 @@
                 ring[b, way, 4, k] = send(buf.at[slot], buf.at[slot], at(dz=way * 2))
             ring[b, way, 3, k] = send(buf.at[slot], buf.at[slot], at(dz=way))
 
-    def all_rows(b, pieces):
-        for k in pieces:
+    def all_rows(b):
+        for k in range(YH):
             for way in (1, -1):
-                if b == 1 or k != 0:
-                    ring[b, way, 1, k].wait_recv()
-                    ring[b, way, 3, k].wait_recv()
-                    if (b, way, 4, k) in ring:
-                        ring[b, way, 4, k].wait_recv()
+                ring[b, way, 1, k].wait_recv()
+                ring[b, way, 3, k].wait_recv()
+                if (b, way, 4, k) in ring:
+                    ring[b, way, 4, k].wait_recv()
 
     y_tok = {}
+    shifts = (4, 3, -3, 2, -2, 1, -1)
+    z_tok = {}
+
+    def to_all_z(src, k):
+        slot = z * YH + y_slot(k)
+        for shift in shifts:
+            z_tok[shift, k] = send(src, x_tok.at[slot], at(dz=shift))
+
     y_tok[0, 2] = send(tok_in, x_tok.at[dp], at(dyh=2))
-    along_z(0, x_tok, tok_in, 0)
+    to_all_z(tok_in, 0)
     for k in (1, 3):
         y_tok[0, k] = send(tok_in, x_tok.at[dp], at(dyh=k))
     y_grd = {k: send(grd_in, x_grd.at[dp], at(dyh=k)) for k in (2, 1, 3)}
@@ -125,21 +132,15 @@
         for k in (1, 3):
             y_tok[shift, k] = send(x_tok.at[slot], x_tok.at[slot], at(dyh=k))
 
-    for way in (1, -1):
-        ring[0, way, 1, 0].wait_recv()
-        to_neighbours(way)
-    pass_along_z(0, x_tok, 0)
-    to_neighbours(2)
-    to_neighbours(-2)
+    for shift in (1, -1, 2, -2):
+        z_tok[shift, 0].wait_recv()
+        to_neighbours(shift)
     y_tok[0, 2].wait_recv()
-    along_z(0, x_tok, x_tok.at[z * YH + y_slot(2)], 2)
+    to_all_z(x_tok.at[z * YH + y_slot(2)], 2)
+    for shift in (3, -3, 4):
+        z_tok[shift, 0].wait_recv()
+        to_neighbours(shift)
     along_z(1, x_grd, grd_in, 0)
-    for way in (1, -1):
-        ring[0, way, 3, 0].wait_recv()
-        to_neighbours(way * 3)
-    ring[0, 1, 4, 0].wait_recv()
-    to_neighbours(4)
-    pass_along_z(0, x_tok, 2)
     for k in (1, 3, 2):
         y_grd[k].wait_recv()
         along_z(1, x_grd, x_grd.at[z * YH + y_slot(k)], k)
@@ -167,15 +168,22 @@
     def spread(pairs, total, pr, cs, us, cr, ur):
         for pair_copy in pairs:
             pair_copy.wait_recv()
+        largest = {}
+        for dx, dyl in chip_peers:
+            q = in_group(dx, dyl, 0) // CORES
+            for i in range(total.shape[0]):
+                summed = total[i, rows_of_chip(q)] + pr[i, rows_of_chip(q)]
+                total[i, rows_of_chip(q)] = summed
+                most = jnp.max(jnp.max(jnp.abs(summed), axis=0, keepdims=True), axis=1, keepdims=True)
+                largest[dx, dyl, i] = jnp.maximum(most, 1e-30)
         copies = []
         for n, (dx, dyl) in enumerate(chip_peers):
             there = in_group(dx, dyl, 0)
             q = there // CORES
             for i in range(total.shape[0]):
-                summed = total[i, rows_of_chip(q)] + pr[i, rows_of_chip(q)]
-                most = jnp.maximum(jnp.max(jnp.abs(summed)), 1e-30)
-                us[q, i] = jnp.full((8, 128), most * (1.0 / (LEVELS * LEVELS)), f32)
-                cs[q, i] = encode(summed, most)
+                most = largest[dx, dyl, i]
+                us[q, i] = jnp.broadcast_to(most * (1.0 / (LEVELS * LEVELS)), (8, 128))
+                cs[q, i] = encode(total[i, rows_of_chip(q)], most)
             copies.append((send(us.at[q], ur.at[n], (dp, there)), send(cs.at[q], cr.at[n], (dp, there))))
         return copies
 
@@ -188,7 +196,8 @@
                 mine[i] += decode(cr[n, i], ur[n, i, 0:1, 0:1])
         return mine
 
-    all_rows(0, (2,))
+    for shift in reversed(shifts):
+        z_tok[shift, 2].wait_recv()
     for shift in (0, 1, -1, 2, -2, 3, -3, 4):
         for k in (1, 3):
             y_tok[shift, k].wait_recv()
@@ -198,7 +207,7 @@
     for i, weight in enumerate((wg, wu)):
         sum_act[i] = product(x_tok, core, weight)
     c_act = spread(pairs, sum_act, pr_act, cs_act, us_act, cr_act, ur_act)
-    all_rows(1, range(YH))
+    all_rows(1)
     pairs = for_other(x_grd, (wd,), ps_grd, pr_grd)
     sum_grd[0] = product(x_grd, core, wd)
     c_grd = spread(pairs, sum_grd, pr_grd, cs_grd, us_grd, cr_grd, ur_grd)
@@ -227,6 +236,17 @@
             copy.wait_recv()
             slot = in_group(far_x[n % 3], n // 3, 0, sign=-1)
             second.append(send(own.at[slot], own.at[slot], other))
+
+    def straight_down(far, k, e_z):
+        slot = y_slot(k)
+        for d in (4, 3, 2, 1):
+            e_z[d, k] = send(far.at[slot], far.at[d * YH + slot], at(dz=-d), None if d < 4 or k == 0 else slot <= yh)
+
+    def over_y(far, e_y, hop):
+        slot = hop * YH + yh
+        for k in (1, 3):
+            only = {0: (yh + k) % YH < yh, 4: (yh + k) % YH > yh}.get(hop)
+            e_y[hop, k] = send(far.at[slot], far.at[slot], at(dyh=k), only)
 
     def down_z(far, through, k, e_z):
         slot = y_slot(k)
@@ -249,9 +269,10 @@
     hidden = (gate / (1.0 + jnp.exp(-gate)) * up).astype(bf16)
     own_act[tensor] = hidden
     far_act[yh] = hidden
-    act_y = {k: send(far_act.at[yh], far_act.at[yh], at(dyh=k)) for k in (2, 1, 3)}
-    act_z = {}
-    down_z(far_act, pass_act, 0, act_z)
+    act_z, act_y = {}, {}
+    act_opposite = send(far_act.at[yh], far_act.at[yh], at(dyh=2))
+    straight_down(far_act, 0, act_z)
+    over_y(far_act, act_y, 0)
     d_act = share_out(own_act)
 
     (grad_sum,) = gathered(c_grd, sum_grd, pr_grd, cr_grd, ur_grd)
@@ -259,33 +280,32 @@
     own_grd[tensor] = hidden_grad
     far_grd[yh] = hidden_grad
     grd_z, grd_y = {}, {}
+    grd_opposite = send(far_grd.at[yh], far_grd.at[yh], at(dyh=2))
     down_z(far_grd, pass_grd, 0, grd_z)
-    for k in (2, 1, 3):
-        grd_y[0, k] = send(far_grd.at[yh], far_grd.at[yh], at(dyh=k), (yh + k) % YH < yh)
+    over_y(far_grd, grd_y, 0)
     d_grd = share_out(own_grd)
 
-    def over_y(hop):
-        slot = hop * YH + yh
-        for k in (2, 1, 3):
-            grd_y[hop, k] = send(far_grd.at[slot], far_grd.at[slot], at(dyh=k), None if hop < 4 else (yh + k) % YH > yh)
-
-    pass_down_z(far_act, pass_act, 0, act_z)
-    for k in (1, 3, 2):
-        act_y[k].wait_recv()
-        down_z(far_act, pass_act, k, act_z)
+    for hop in (1, 2):
+        act_z[hop, 0].wait_recv()
+        over_y(far_act, act_y, hop)
+    act_opposite.wait_recv()
+    straight_down(far_act, 2, act_z)
+    for hop in (3, 4):
+        act_z[hop, 0].wait_recv()
+        over_y(far_act, act_y, hop)
     grd_z[1, 0].wait_recv()
-    over_y(1)
+    over_y(far_grd, grd_y, 1)
     pass_down_z(far_grd, pass_grd, 0, grd_z)
-    over_y(2)
+    over_y(far_grd, grd_y, 2)
+    grd_opposite.wait_recv()
+    down_z(far_grd, pass_grd, 2, grd_z)
     pass_across(own_act, *d_act)
     pass_across(own_grd, *d_grd)
-    for k in (1, 3, 2):
-        pass_down_z(far_act, pass_act, k, act_z)
     for hop in (3, 4):
         grd_z[hop, 0].wait_recv()
-        over_y(hop)
+        over_y(far_grd, grd_y, hop)
+    pass_down_z(far_grd, pass_grd, 2, grd_z)
     pass_on(own_act, *d_act)
-    pass_on(own_grd, *d_grd)
 
     def deliver(far, st, b):
         for j in range(GROUP):
@@ -294,20 +314,22 @@
         b[tensor] = st[tensor]
         return copies
 
-    for k in range(YH):
-        act_z[1, k].wait_recv()
-        act_z[3, k].wait_recv()
-        if k == 0:
-            act_z[4, k].wait_recv()
-        else:
-            pl.when(y_slot(k) <= yh)(act_z[4, k].wait_recv)
+    def all_far(e_z, e_y, steps):
+        for step in steps:
+            e_z[step, 2].wait_recv()
+        pl.when(y_slot(2) <= yh)(e_z[4, 2].wait_recv)
+        for k in (1, 3):
+            there = y_slot(k)
+            pl.when(yh < there)(e_y[0, k].wait_recv)
+            for hop in (1, 2, 3):
+                e_y[hop, k].wait_recv()
+            pl.when(yh > there)(e_y[4, k].wait_recv)
+
+    all_far(act_z, act_y, (1, 2, 3))
+    before = len(sent)
     e_act = deliver(far_act, st_act, b_act)
-    for k in (1, 2, 3):
-        there = y_slot(k)
-        pl.when(yh < there)(grd_y[0, k].wait_recv)
-        for hop in (1, 2, 3):
-            grd_y[hop, k].wait_recv()
-        pl.when(yh > there)(grd_y[4, k].wait_recv)
+    pass_on(own_grd, *d_grd)
+    all_far(grd_z, grd_y, (1, 3))
     e_grd = deliver(far_grd, st_grd, b_grd)
 
     diagonal = (distance == DP // 2) & (dp >= DP // 2)
@@ -327,6 +349,14 @@
         take_lower = jnp.where(p > q, jnp.where(is_diagonal, 1, 0), 0) == 1
         out[...] = jnp.where(take_lower, lower, upper) * (1.0 / (DP * 16))
 
+    def finish(copies):
+        for only, copy in copies:
+            if only is None:
+                copy.wait_send()
+            else:
+                pl.when(only)(copy.wait_send)
+
+    finish(sent[:before])
     tile(own_act, b_act, d_act[2], e_act, tile_act)
     write_act = pltpu.make_async_copy(tile_act, act_out.at[0], local_sem.at[1])
     write_act.start()
@@ -334,13 +364,26 @@
     write_grd = pltpu.make_async_copy(tile_grd, grad_out.at[0], local_sem.at[2])
     write_grd.start()
 
-    for only, copy in sent:
-        if only is None:
-            copy.wait_send()
-        else:
-            pl.when(only)(copy.wait_send)
+    finish(sent[before:])
     write_act.wait()
     write_grd.wait()
+
+
+def hand_over(act, grad, act_out, grad_out, held, load_sems, store_sems):
+    parts, rows = held.shape[1], held.shape[2]
+    loads, stores = [], []
+    for i, (source, target) in enumerate(((act, act_out), (grad, grad_out))):
+        for n in range(parts):
+            part = pl.ds(n * rows, rows)
+            loads.append(pltpu.make_async_copy(source.at[0, part], held.at[i, n], load_sems.at[i, n]))
+            stores.append(pltpu.make_async_copy(held.at[i, n], target.at[0, part], store_sems.at[i, n]))
+    for load in loads:
+        load.start()
+    for load, store in zip(loads, stores):
+        load.wait()
+        store.start()
+    for store in stores:
+        store.wait()
 
 
 def local(tokens, out_grad, gate_weight, up_weight, down_weight, pair_list):
@@ -349,6 +392,7 @@
     half = rows * DP // 4
     piece = half // CHIPS
     any_space = pl.BlockSpec(memory_space=pl.ANY)
+    hbm = pl.BlockSpec(memory_space=pltpu.HBM)
     tile = jax.ShapeDtypeStruct((1, width, width), f32)
 
     def vmem(shape, kind):
@@ -367,22 +411,31 @@
         vmem((CHIPS, 1, 8, 128), f32), vmem((CHIPS - 1, 1, 8, 128), f32),
         vmem((GROUP, piece, 2 * width), bf16), vmem((GROUP, piece, 2 * width), bf16),
         vmem((5 * YH, piece, 2 * width), bf16), vmem((5 * YH, piece, 2 * width), bf16),
-        vmem((YH, piece, 2 * width), bf16), vmem((YH, piece, 2 * width), bf16),
+        vmem((YH, piece, 2 * width), bf16),
         vmem((GROUP, piece, 2 * width), bf16), vmem((GROUP, piece, 2 * width), bf16),
         vmem((GROUP, piece, 2 * width), bf16), vmem((GROUP, piece, 2 * width), bf16),
         vmem((width, width), f32), vmem((width, width), f32),
         pltpu.SemaphoreType.DMA((5,)), pltpu.SemaphoreType.DMA((256,)), pltpu.SemaphoreType.DMA((256,)),
     ]
-    return pl.pallas_call(
+    tiles = pl.pallas_call(
         kernel,
         out_shape=(tile, tile),
-        in_specs=[any_space] * 5 + [pl.BlockSpec(memory_space=pltpu.SMEM)],
+        in_specs=[hbm] * 5 + [pl.BlockSpec(memory_space=pltpu.SMEM)],
         out_specs=(any_space, any_space),
         scratch_shapes=scratch,
         compiler_params=pltpu.CompilerParams(
             collective_id=0, has_side_effects=True, vmem_limit_bytes=60 * 1024 * 1024),
         name="covariance",
     )(tokens, out_grad, gate_weight.T, up_weight.T, down_weight, pair_list)
+    return pl.pallas_call(
+        hand_over,
+        out_shape=(tile, tile),
+        in_specs=[hbm, hbm],
+        out_specs=(hbm, hbm),
+        scratch_shapes=[vmem((2, 4, width // 4, width), f32), pltpu.SemaphoreType.DMA((2, 4)), pltpu.SemaphoreType.DMA((2, 4))],
+        compiler_params=pltpu.CompilerParams(vmem_limit_bytes=60 * 1024 * 1024),
+        name="results",
+    )(*tiles)
 
 
 def solution(mesh):

time: 79.5 us -> 75.6 us (0.951)
  local copies, waits for them, and re-layouts: 3.17 us -> 0 us
    unnamed x4 -> x0, local copies, waits for them, and re-layouts: 3.17 us -> none
    pallas_call x1 -> x2, Pallas kernels: 75.5 us -> 74.8 us  [the longest x1 72.4 us: local(): pl.pallas_call(kernel, out_shape=(tile, tile), in_specs=[hbm] * 5 + [pl.B...]
where the time goes in v3:
time: 75.6 us; the launch traced here: 75.4 us
  Pallas kernels  74.8 us (99%)
    pallas_call x1, Pallas kernels, local(): pl.pallas_call(kernel, out_shape=(tile, tile), in_specs=[hbm] * 5 + [pl.B...  72.4 us
    pallas_call x1, Pallas kernels, local(): pl.pallas_call(hand_over, out_shape=(tile, tile), in_specs=[hbm, hbm], ou...  2.41 us

profile of v3, /device:TPU:1, one launch (start us, length us, event | category | flops | bytes accessed | tf_op | source)
XLA Modules:
  0.0 75.4 jit_solution(4692744251487447306)
XLA Ops:
  0.6 72.4 %covariance.1 = (f32[1,448,448]{2,1,0:T(8,128)}, f32[1,448,448]{2,1,0:T(8,128)}) custom-call(bf16[16,512]{1,0:T(8,128)(2,1)} %tok_in.1, bf16[16,512]{1,0:T(8,128)(2,1)} %grd_in.1, bf16[448,512]{1,0:T(8,128)(2,1)} %bitcast.2, bf16[448,512]{1,0:T(8,128)(2,1)} %bitcast.3, bf16[448,512]{1,0:T(8,128)(2,1)} %wd_in.1, s32[1,2]{1,0:T(1,128)} %pair.1), custom_call_target="tpu_custom_call" | custom-call | tf_op jit(solution)/shard_map/covariance/pallas_call | solution.py:420
  73.0 2.4 %results.1 = (f32[1,448,448]{2,1,0:T(8,128)}, f32[1,448,448]{2,1,0:T(8,128)}) custom-call(f32[1,448,448]{2,1,0:T(8,128)} %get-tuple-element.4.act, f32[1,448,448]{2,1,0:T(8,128)} %get-tuple-element.5.grad), custom_call_target="tpu_custom_call" | custom-call | tf_op jit(solution)/shard_map/results/pallas_call | solution.py:430

commit v4 on v3

--- a/solution.py
+++ b/solution.py
@@ -67,8 +67,8 @@
         sent.append((only, copy))
         return copy
 
-    peers = [(dx, dyl, dc) for dx in (2, 1, 3, 0) for dyl in (1, 0) for dc in (0, 1) if (dx, dyl, dc) != (0, 0, 0)]
-    chip_peers = [(dx, dyl) for dx in (2, 1, 3, 0) for dyl in (1, 0) if (dx, dyl) != (0, 0)]
+    peers = [(dx, dyl, dc) for dyl in (1, 0) for dx in (2, 1, 3, 0) for dc in (0, 1) if (dx, dyl, dc) != (0, 0, 0)]
+    chip_peers = [(dx, dyl) for dyl in (1, 0) for dx in (2, 1, 3, 0) if (dx, dyl) != (0, 0)]
 
     barrier = pltpu.get_barrier_semaphore()
     partners = [at(dyh=k) for k in (1, 2, 3)] + [at(dz=k) for k in (1, -1, 2, -2, 3, -3, 4)] + [(dp, in_group(*o)) for o in peers]
@@ -126,6 +126,8 @@
     for k in (1, 3):
         y_tok[0, k] = send(tok_in, x_tok.at[dp], at(dyh=k))
     y_grd = {k: send(grd_in, x_grd.at[dp], at(dyh=k)) for k in (2, 1, 3)}
+    along_z(1, x_grd, grd_in, 0)
+    pair_copies = [send(pair_tiles.at[tensor], pair_tiles.at[tensor], (dp, in_group(*o))) for o in peers]
 
     def to_neighbours(shift):
         slot = (z - shift + Z) % Z * YH + yh
@@ -137,14 +139,12 @@
         to_neighbours(shift)
     y_tok[0, 2].wait_recv()
     to_all_z(x_tok.at[z * YH + y_slot(2)], 2)
+    for k in (1, 3, 2):
+        y_grd[k].wait_recv()
+        along_z(1, x_grd, x_grd.at[z * YH + y_slot(k)], k)
     for shift in (3, -3, 4):
         z_tok[shift, 0].wait_recv()
         to_neighbours(shift)
-    along_z(1, x_grd, grd_in, 0)
-    for k in (1, 3, 2):
-        y_grd[k].wait_recv()
-        along_z(1, x_grd, x_grd.at[z * YH + y_slot(k)], k)
-    pair_copies = [send(pair_tiles.at[tensor], pair_tiles.at[tensor], (dp, in_group(*o))) for o in peers]
     for load in loads:
         load.wait()
 
@@ -196,13 +196,14 @@
                 mine[i] += decode(cr[n, i], ur[n, i, 0:1, 0:1])
         return mine
 
+    pass_along_z(1, x_grd, 0)
     for shift in reversed(shifts):
         z_tok[shift, 2].wait_recv()
     for shift in (0, 1, -1, 2, -2, 3, -3, 4):
         for k in (1, 3):
             y_tok[shift, k].wait_recv()
     pairs = for_other(x_tok, (wg, wu), ps_act, pr_act)
-    for k in (0, 1, 3, 2):
+    for k in (1, 3, 2):
         pass_along_z(1, x_grd, k)
     for i, weight in enumerate((wg, wu)):
         sum_act[i] = product(x_tok, core, weight)

time: 75.6 us -> 75.7 us (level)
  no operation moved by 1% of the time
where the time goes in v4:
time: 75.7 us; the launch traced here: 75.1 us
  Pallas kernels  74.5 us (98%)
    pallas_call x1, Pallas kernels, local(): pl.pallas_call(kernel, out_shape=(tile, tile), in_specs=[hbm] * 5 + [pl.B...  72.1 us
    pallas_call x1, Pallas kernels, local(): pl.pallas_call(hand_over, out_shape=(tile, tile), in_specs=[hbm, hbm], ou...  2.41 us

profile of v4, /device:TPU:1, one launch (start us, length us, event | category | flops | bytes accessed | tf_op | source)
XLA Modules:
  0.0 75.1 jit_solution(8669086955222006474)
XLA Ops:
  0.6 72.1 %covariance.1 = (f32[1,448,448]{2,1,0:T(8,128)}, f32[1,448,448]{2,1,0:T(8,128)}) custom-call(bf16[16,512]{1,0:T(8,128)(2,1)} %tok_in.1, bf16[16,512]{1,0:T(8,128)(2,1)} %grd_in.1, bf16[448,512]{1,0:T(8,128)(2,1)} %bitcast.2, bf16[448,512]{1,0:T(8,128)(2,1)} %bitcast.3, bf16[448,512]{1,0:T(8,128)(2,1)} %wd_in.1, s32[1,2]{1,0:T(1,128)} %pair.1), custom_call_target="tpu_custom_call" | custom-call | tf_op jit(solution)/shard_map/covariance/pallas_call | solution.py:421
  72.7 2.4 %results.1 = (f32[1,448,448]{2,1,0:T(8,128)}, f32[1,448,448]{2,1,0:T(8,128)}) custom-call(f32[1,448,448]{2,1,0:T(8,128)} %get-tuple-element.4.act, f32[1,448,448]{2,1,0:T(8,128)} %get-tuple-element.5.grad), custom_call_target="tpu_custom_call" | custom-call | tf_op jit(solution)/shard_map/results/pallas_call | solution.py:431
